TPU v7x, 32 devices: a whole 2x2x4 slice. The times are simulated.
32 devices in a mesh: groups: 2 (over y), patch: 4 (over z), feat: 2 (over x), sub: 2 (over core).
Axes of the slice: x: 2, y: 2, z: 4, core: 2. Of those that a mesh axis runs over, the one named last changes fastest.
Arguments:
- grid_feat: bfloat16 [32768, 512], P(('groups', 'patch', 'feat', 'sub')), parts along dimension 0, may hold values from -6 to 6
- block_owner: int32 [256], P(('groups', 'patch', 'feat', 'sub')), parts along dimension 0, may hold values from 0 to 3, as said below
- enc_node: int32 [32768], P(('groups', 'patch', 'feat', 'sub')), parts along dimension 0, may hold values from 0 to 31
- dec_node: int32 [32768], P(('groups', 'patch', 'feat', 'sub')), parts along dimension 0, may hold values from 0 to 31
- mesh_feat: bfloat16 [1024, 512], P(('groups', 'patch', 'feat', 'sub')), parts along dimension 0, may hold values from -6 to 6
- edge_feat: bfloat16 [8192, 512], P(('groups', 'patch', 'feat', 'sub')), parts along dimension 0, may hold values from -6 to 6
- senders: int32 [8192], P(('groups', 'patch', 'feat', 'sub')), parts along dimension 0, may hold values from 0 to 191
- receivers: int32 [8192], P(('groups', 'patch', 'feat', 'sub')), parts along dimension 0, may hold values from 0 to 31
- enc_w1: bfloat16 [512, 512], P(('feat', 'sub')), may hold values from -0.25 to 0.25
- enc_w2: bfloat16 [512, 512], P(('feat', 'sub')), may hold values from -0.25 to 0.25
- gn_w1: bfloat16 [1024, 512], P(('feat', 'sub')), may hold values from -0.1875 to 0.1875
- gn_w2: bfloat16 [512, 512], P(('feat', 'sub')), may hold values from -0.25 to 0.25
- edge_w1: bfloat16 [1536, 512], P(('feat', 'sub')), may hold values from -0.15625 to 0.15625
- edge_w2: bfloat16 [512, 512], P(('feat', 'sub')), may hold values from -0.25 to 0.25
- node_w1: bfloat16 [1024, 512], P(('feat', 'sub')), may hold values from -0.1875 to 0.1875
- node_w2: bfloat16 [512, 512], P(('feat', 'sub')), may hold values from -0.25 to 0.25
- dec_w1: bfloat16 [1024, 512], P(('feat', 'sub')), may hold values from -0.1875 to 0.1875
- dec_w2: bfloat16 [512, 512], P(('feat', 'sub')), may hold values from -0.25 to 0.25
Outputs:
- grid_out: bfloat16 [32768, 512], P(('groups', 'patch', 'feat', 'sub')), parts along dimension 0
There are 2 independent parts, one for each index of `groups`. A program takes and returns all parts, laid end to end along the dimension named above; an argument that names none is the same for every part. Nothing has to cross between parts.
Inputs may be any that keep to these rules, and one draw needn't show every extreme that they name: `block_owner`: among the 8 blocks of one device along patch+feat+sub (aligned runs of 8 entries), at most 2 name the same patch, and one patch is named by exactly 2 blocks of every device.
All inputs are finite; a program needn't handle non-finite values.
Results may differ from a plain program's by a relative error of at most 0.015.
Values may be sent and summed in bfloat16 or wider, within the bound.
A program may use at most 64 MiB of HBM per device.

v0:
```python
import jax
import jax.numpy as jnp
from jax import lax
from jax.sharding import PartitionSpec as P

BND = 32


def extended_2(array, sides, width):
    for axis, dim in sides:
        size, length = (lax.axis_size(axis), array.shape[dim])
        up = [(i, (i + 1) % size) for i in range(size)]
        down = [(j, i) for i, j in up]
        last = lax.slice_in_dim(array, length - width, length, axis=dim)
        first = lax.slice_in_dim(array, 0, width, axis=dim)
        before = lax.ppermute(last, axis, up)
        after = lax.ppermute(first, axis, down)
        array = jnp.concatenate([before, array, after], axis=dim)
    return array


def layer_norm(values):
    centred = values - jnp.mean(values, axis=-1, keepdims=True)
    spread = jnp.mean(centred * centred, axis=-1, keepdims=True)
    return centred * lax.rsqrt(spread + 1e-05)


def network(inputs, first, second):
    hidden = jax.nn.silu(jnp.dot(inputs, first, preferred_element_type=jnp.float32)).astype(
        jnp.bfloat16
    )
    return layer_norm(jnp.dot(hidden, second, preferred_element_type=jnp.float32))


def owner_slots(block_owner, patch_count, capacity):
    owner_hot = (block_owner[:, None] == jnp.arange(patch_count, dtype=jnp.int32)[None, :]).astype(
        jnp.int32
    )
    earlier = jnp.cumsum(owner_hot, axis=0) - owner_hot
    return block_owner * capacity + jnp.sum(earlier * owner_hot, axis=1)


def per_device(
    grid_feat,
    block_owner,
    enc_node,
    dec_node,
    mesh_feat,
    edge_feat,
    senders,
    receivers,
    enc_w1,
    enc_w2,
    gn_w1,
    gn_w2,
    edge_w1,
    edge_w2,
    node_w1,
    node_w2,
    dec_w1,
    dec_w2,
):
    (
        full_enc1,
        full_enc2,
        full_gn1,
        full_gn2,
        full_edge1,
        full_edge2,
        full_node1,
        full_node2,
        full_dec1,
        full_dec2,
    ) = (
        lax.all_gather(enc_w1, ("feat", "sub"), axis=0, tiled=True),
        lax.all_gather(enc_w2, ("feat", "sub"), axis=0, tiled=True),
        lax.all_gather(gn_w1, ("feat", "sub"), axis=0, tiled=True),
        lax.all_gather(gn_w2, ("feat", "sub"), axis=0, tiled=True),
        lax.all_gather(edge_w1, ("feat", "sub"), axis=0, tiled=True),
        lax.all_gather(edge_w2, ("feat", "sub"), axis=0, tiled=True),
        lax.all_gather(node_w1, ("feat", "sub"), axis=0, tiled=True),
        lax.all_gather(node_w2, ("feat", "sub"), axis=0, tiled=True),
        lax.all_gather(dec_w1, ("feat", "sub"), axis=0, tiled=True),
        lax.all_gather(dec_w2, ("feat", "sub"), axis=0, tiled=True),
    )
    width = grid_feat.shape[1]
    block_count = block_owner.shape[0]
    block_rows = grid_feat.shape[0] // block_count
    node_count = mesh_feat.shape[0]
    patch_count = lax.axis_size("patch")
    capacity = (block_count + patch_count - 1) // patch_count
    node_ids = jnp.arange(node_count, dtype=jnp.int32)
    slot = owner_slots(block_owner, patch_count, capacity)
    buffer = (
        jnp.zeros((patch_count * capacity, block_rows, width), jnp.bfloat16)
        .at[slot]
        .set(grid_feat.reshape(block_count, block_rows, width))
    )
    slot_nodes = (
        jnp.full((patch_count * capacity, block_rows), -1, jnp.int32)
        .at[slot]
        .set(enc_node.reshape(block_count, block_rows))
    )
    arrived, arrived_nodes = (
        lax.all_to_all(
            buffer.reshape(patch_count, capacity * block_rows, width),
            "patch",
            split_axis=0,
            concat_axis=0,
            tiled=True,
        ),
        lax.all_to_all(
            slot_nodes.reshape(patch_count, capacity * block_rows),
            "patch",
            split_axis=0,
            concat_axis=0,
            tiled=True,
        ),
    )
    arrived = arrived.reshape(-1, width)
    messages = network(arrived, full_enc1, full_enc2).astype(jnp.bfloat16)
    selector = (node_ids[:, None] == arrived_nodes.reshape(-1)[None, :]).astype(jnp.bfloat16)
    gathered = jnp.dot(selector, messages, preferred_element_type=jnp.float32)
    gathered_half = gathered.astype(jnp.bfloat16)
    mesh_mid = (
        mesh_feat + network(jnp.concatenate([mesh_feat, gathered_half], 1), full_gn1, full_gn2)
    ).astype(jnp.bfloat16)
    patch_mesh = lax.all_gather(mesh_mid, ("feat", "sub"), axis=0, tiled=True)
    extended = extended_2(patch_mesh, (("patch", 0),), BND)
    edge_inputs = jnp.concatenate([edge_feat, extended[senders], mesh_mid[receivers]], 1)
    edge_new = (edge_feat + network(edge_inputs, full_edge1, full_edge2)).astype(jnp.bfloat16)
    incoming = (node_ids[:, None] == receivers[None, :]).astype(jnp.bfloat16)
    edge_sum = jnp.dot(incoming, edge_new, preferred_element_type=jnp.float32).astype(jnp.bfloat16)
    mesh_out = (
        mesh_mid + network(jnp.concatenate([mesh_mid, edge_sum], 1), full_node1, full_node2)
    ).astype(jnp.bfloat16)
    lane_mesh = lax.all_gather(mesh_out, "patch", axis=0, tiled=True)
    source = (
        block_owner[:, None] * node_count + dec_node.reshape(block_count, block_rows)
    ).reshape(-1)
    decoder_in = jnp.concatenate([grid_feat, lane_mesh[source]], 1)
    return (grid_feat + network(decoder_in, full_dec1, full_dec2)).astype(jnp.bfloat16)


def solution(mesh):
    in_specs = (
        P(("groups", "patch", "feat", "sub"), None),
        P(("groups", "patch", "feat", "sub")),
        P(("groups", "patch", "feat", "sub")),
        P(("groups", "patch", "feat", "sub")),
        P(("groups", "patch", "feat", "sub"), None),
        P(("groups", "patch", "feat", "sub"), None),
        P(("groups", "patch", "feat", "sub")),
        P(("groups", "patch", "feat", "sub")),
        P(("feat", "sub"), None),
        P(("feat", "sub"), None),
        P(("feat", "sub"), None),
        P(("feat", "sub"), None),
        P(("feat", "sub"), None),
        P(("feat", "sub"), None),
        P(("feat", "sub"), None),
        P(("feat", "sub"), None),
        P(("feat", "sub"), None),
        P(("feat", "sub"), None),
    )
    out_specs = P(("groups", "patch", "feat", "sub"), None)
    return jax.shard_map(
        per_device, mesh=mesh, in_specs=in_specs, out_specs=out_specs, check_vma=False
    )
```

profile of v0, /device:TPU:0, one launch (start us, length us, event | category | flops | bytes accessed | tf_op | source)
XLA Modules:
  0.0 138.7 jit_solution(18227705283891680364)
XLA Ops:
  6.5 0.0 copy-start
  6.5 0.0 all-gather.5.cloned.1.call-start
  6.5 0.7 all-gather.5.cloned.1.call-update
  7.3 0.0 all-gather.7.cloned.1.call-start
  7.3 0.7 all-gather.7.cloned.1.call-update
  8.0 0.0 all-gather.9.cloned.1.call-start
  8.1 0.7 all-gather.9.cloned.1.call-update
  8.7 0.7 fusion.51
  9.4 0.2 reduce_window_sum.11
  9.6 0.7 select_reduce_fusion
  10.3 0.7 broadcast_multiply_fusion.3
  10.9 1.1 broadcast_in_dim.14
  12.0 0.0 copy-done.1
  12.0 2.8 %scatter_fusion = bf16[8,128,512]{2,1,0:T(8,128)(2,1)} fusion(bf16[8,128,512]{2,1,0:T(8,128)(2,1)} %broadcast_in_dim.14, s32[8]{0:T(128)S(1)} %get-tuple-element.8, bf16[8,128,512]{2,1,0:T(8,128)(2,1)S(1)} %bitcast.23), kind=kCustom, calls=%fused_computation.4 | custom fusion | bytes 3145760 | tf_op jit(solution)/shard_map/scatter | solution.py:97
  14.9 6.5 %all-to-all-start.1 = ((bf16[4,256,512]{2,1,0:T(8,128)(2,1)}), bf16[4,256,512]{2,1,0:T(8,128)(2,1)S(1)}, u32[]{:S(2)}, u32[]{:S(2)}) async-start(bf16[4,256,512]{2,1,0:T(8,128)(2,1)} %bitcast.4), calls=%async_computation.1 | async-start | bytes 2097152 | tf_op jit(solution)/shard_map/all_to_all | solution.py:105
  21.3 0.0 all-gather.11.cloned.1.call-start
  21.4 0.5 all-gather.11.cloned.1.call-update
  21.9 0.0 copy-done.15
  21.9 9.1 %all_gather.36 = bf16[512,512]{1,0:T(8,128)(2,1)} all-gather(bf16[128,512]{1,0:T(8,128)(2,1)S(1)} %copy-done.6), channel_id=1, replica_groups=mesh['groups'=2,'patch'=4,'feat'=2,'sub'=2] {'feat','sub'}, dimensions={0}, use_global_device_ids=true | all-gather | bytes 655360 | tf_op jit(solution)/shard_map/all_gather | solution.py:75
  31.0 1.2 scatter_custom_fusion
  32.2 7.7 %all_gather.37 = bf16[512,512]{1,0:T(8,128)(2,1)} all-gather(bf16[128,512]{1,0:T(8,128)(2,1)S(1)} %copy-done.7), channel_id=1, replica_groups=mesh['groups'=2,'patch'=4,'feat'=2,'sub'=2] {'feat','sub'}, dimensions={0}, use_global_device_ids=true | all-gather | bytes 655360 | tf_op jit(solution)/shard_map/all_gather | solution.py:76
  39.9 10.9 %all_gather.39 = bf16[512,512]{1,0:T(8,128)(2,1)} all-gather(bf16[128,512]{1,0:T(8,128)(2,1)S(1)} %copy-done.8), channel_id=1, replica_groups=mesh['groups'=2,'patch'=4,'feat'=2,'sub'=2] {'feat','sub'}, dimensions={0}, use_global_device_ids=true | all-gather | bytes 655360 | tf_op jit(solution)/shard_map/all_gather | solution.py:78
  50.8 7.7 %all_gather.42 = bf16[512,512]{1,0:T(8,128)(2,1)} all-gather(bf16[128,512]{1,0:T(8,128)(2,1)S(1)} %copy-done.9), channel_id=1, replica_groups=mesh['groups'=2,'patch'=4,'feat'=2,'sub'=2] {'feat','sub'}, dimensions={0}, use_global_device_ids=true | all-gather | bytes 655360 | tf_op jit(solution)/shard_map/all_gather | solution.py:80
  58.6 8.4 %all_gather.44 = bf16[512,512]{1,0:T(8,128)(2,1)} all-gather(bf16[128,512]{1,0:T(8,128)(2,1)S(1)} %copy-done.10), channel_id=1, replica_groups=mesh['groups'=2,'patch'=4,'feat'=2,'sub'=2] {'feat','sub'}, dimensions={0}, use_global_device_ids=true | all-gather | bytes 655360 | tf_op jit(solution)/shard_map/all_gather | solution.py:82
  67.0 7.7 %all_gather.47 = bf16[512,512]{1,0:T(8,128)(2,1)} all-gather(bf16[128,512]{1,0:T(8,128)(2,1)S(1)} %copy-done.11), channel_id=1, replica_groups=mesh['groups'=2,'patch'=4,'feat'=2,'sub'=2] {'feat','sub'}, dimensions={0}, use_global_device_ids=true | all-gather | bytes 655360 | tf_op jit(solution)/shard_map/all_gather | solution.py:84
  74.7 0.0 copy-done.13
  74.7 0.1 fusion.48
  74.8 0.0 all-to-all-done.1
  74.8 4.7 %all-to-all-start = ((s32[4,1,256]{2,1,0:T(1,128)}), s32[4,1,256]{2,1,0:T(1,128)S(1)}, u32[]{:S(2)}, u32[]{:S(2)}) async-start(s32[4,1,256]{2,1,0:T(1,128)} %bitcast.1), calls=%async_computation | async-start | bytes 8192 | tf_op jit(solution)/shard_map/all_to_all | solution.py:112
  79.5 3.1 %fusion.67 = (f32[1024]{0:T(1024)S(1)}, f32[1024,512]{0,1:T(8,128)S(1)}) fusion(bf16[512,512]{1,0:T(8,128)(2,1)} %all_gather.37, bf16[1024,512]{1,0:T(8,128)(2,1)} %bitcast.24, bf16[512,512]{1,0:T(8,128)(2,1)} %all_gather.36), kind=kOutput, calls=%fused_computation.92 | convolution fusion | flops 1076886528 | bytes 4198400 | tf_op jit(solution)/shard_map/dot_general | solution.py:32
  82.7 0.0 copy-start.12
  82.7 0.3 multiply_reduce_fusion.1
  83.0 2.1 %all-to-all-done = s32[4,1,256]{2,1,0:T(1,128)S(1)} async-done(((s32[4,1,256]{2,1,0:T(1,128)}), s32[4,1,256]{2,1,0:T(1,128)S(1)}, u32[]{:S(2)}, u32[]{:S(2)}) %all-to-all-start) | async-done | bytes 4128 | tf_op jit(solution)/shard_map/all_to_all | solution.py:112
  85.1 0.4 convolution_convert_fusion.1
  85.5 0.0 all-gather.5.cloned.1.call-done
  85.5 0.0 copy-done.12
  85.6 1.9 %fusion.68 = (f32[32]{0:T(128)S(1)}, f32[32,512]{1,0:T(8,128)S(1)}) fusion(bf16[512,512]{1,0:T(8,128)(2,1)} %all_gather.39, bf16[1024,512]{1,0:T(8,128)(2,1)} %all-gather.5.cloned.1.call-done, bf16[32,512]{1,0:T(8,128)(2,1)S(1)} %convolution_convert_fusion.1, bf16[32,512]{1,0:T(8,128)(2,1)S(1)} %copy-done.12), kind=kOutput, calls=%fused_computation.93 | convolution fusion | flops 50560992 | bytes 1704064 | tf_op jit(solution)/shard_map/dot_general | solution.py:32
  87.5 0.2 multiply_reduce_fusion.4
  87.7 0.1 add_convert_fusion.4
  87.8 5.4 %all_gather.40 = bf16[128,512]{1,0:T(8,128)(2,1)S(1)} all-gather(bf16[32,512]{1,0:T(8,128)(2,1)S(1)} %add_convert_fusion.4), channel_id=1, replica_groups=mesh['groups'=2,'patch'=4,'feat'=2,'sub'=2] {'feat','sub'}, dimensions={0}, use_global_device_ids=true | all-gather | bytes 163840 | tf_op jit(solution)/shard_map/all_gather | solution.py:128
  93.2 0.6 collective-permute-start
  93.8 3.2 %collective-permute-start.1 = (bf16[32,512]{1,0:T(8,128)(2,1)S(1)}, bf16[32,512]{1,0:T(8,128)(2,1)S(1)}, u32[]{:S(2)}, u32[]{:S(2)}) collective-permute-start(bf16[32,512]{1,0:T(8,128)(2,1)S(1)} %get-tuple-element.6), channel_id=1, source_target_pairs={{4,0},{8,4},{12,8},{0,12},{5,1},{9,5},{13,9},{1,13},{6,2},{10,6},{... | collective-permute-start | bytes 98312 | tf_op jit(solution)/shard_map/ppermute | solution.py:17
  97.1 1.3 copy.23
  98.4 1.2 gather_fusion.1
  99.5 0.0 collective-permute-done
  99.5 0.0 collective-permute-done.1
  99.6 1.2 gather_fusion
  100.7 0.0 all-gather.7.cloned.1.call-done
  100.8 0.0 copy-done.5
  100.8 2.5 %fusion.71 = (f32[256]{0:T(256)S(1)}, f32[256,512]{1,0:T(8,128)S(1)}) fusion(bf16[512,512]{1,0:T(8,128)(2,1)S(1)} %copy-done.5, bf16[1536,512]{1,0:T(8,128)(2,1)} %all-gather.7.cloned.1.call-done, bf16[256,512]{1,0:T(8,128)(2,1)S(1)} %gather_fusion.1, bf16[256,512]{1,0:T(8,128)(2,1)S(1)} %gather_fusion, bf16[256,512]{1,0:T(8,128)(2,1)} %param.23), kind=kOutput, calls=%fused_computation.94 | convolution fusion | flops 540016384 | bytes 3408896 | tf_op jit(solution)/shard_map/dot_general | solution.py:32
  103.3 0.2 multiply_reduce_fusion.2
  103.5 1.2 convolution_convert_fusion
  104.7 0.0 all-gather.9.cloned.1.call-done
  104.8 1.8 %fusion.74 = (f32[32]{0:T(128)S(1)}, f32[32,512]{1,0:T(8,128)S(1)}) fusion(bf16[512,512]{1,0:T(8,128)(2,1)S(1)} %copy-done.3, bf16[1024,512]{1,0:T(8,128)(2,1)} %all-gather.9.cloned.1.call-done, bf16[32,512]{1,0:T(8,128)(2,1)S(1)} %convolution_convert_fusion, bf16[32,512]{1,0:T(8,128)(2,1)S(1)} %add_convert_fusion.4), kind=kOutput, calls=%fused_computation.95 | convolution fusion | flops 50560992 | bytes 1704064 | tf_op jit(solution)/shard_map/dot_general | solution.py:32
  106.6 0.2 multiply_reduce_fusion.3
  106.8 0.1 add_convert_fusion.3
  106.9 13.5 %all_gather.45 = bf16[128,512]{1,0:T(8,128)(2,1)S(1)} all-gather(bf16[32,512]{1,0:T(8,128)(2,1)S(1)} %add_convert_fusion.3), channel_id=1, replica_groups=mesh['groups'=2,'patch'=4,'feat'=2,'sub'=2] {'patch'}, dimensions={0}, use_global_device_ids=true | all-gather | bytes 163840 | tf_op jit(solution)/shard_map/all_gather | solution.py:137
  120.3 5.0 %gather_fusion.2 = bf16[1024,512]{1,0:T(8,128)(2,1)} fusion(bf16[128,512]{1,0:T(8,128)(2,1)S(1)} %all_gather.45, s32[1024]{0:T(1024)S(1)} %fusion.48), kind=kCustom, calls=%fused_computation.2 | custom fusion | bytes 2101248 | tf_op jit(solution)/shard_map/gather | solution.py:141
  125.4 3.7 %fusion.77 = (f32[1024]{0:T(1024)S(1)}, f32[1024,512]{0,1:T(8,128)S(1)}) fusion(bf16[512,512]{1,0:T(8,128)(2,1)} %all_gather.47, bf16[1024,512]{1,0:T(8,128)(2,1)} %all-gather.11.cloned.1.call-done, bf16[1024,512]{1,0:T(8,128)(2,1)} %gather_fusion.2, bf16[1024,512]{1,0:T(8,128)(2,1)S(1)} %copy-done.1), kind=kOutput, calls=%fused_computation.96 | convolution fusion | flops 1617951744 | bytes 5771264 | tf_op jit(solution)/shard_map/dot_general | solution.py:32
  129.1 0.0 copy-start.2
  129.2 0.3 multiply_reduce_fusion
  129.5 0.9 copy-done.2
  130.4 0.4 add_convert_fusion
  130.8 1.3 copy.24
  (40 shorter events, 0.1 us)
Async XLA Ops:
  6.5 24.5 %copy-start = (s32[1024]{0:T(1024)S(1)}, s32[1024]{0:T(1024)}, u32[]{:S(2)}) copy-start(s32[1024]{0:T(1024)} %param.20) | copy-start | bytes 12292
  6.5 5.5 %copy-start.1 = (bf16[1024,512]{1,0:T(8,128)(2,1)S(1)}, bf16[1024,512]{1,0:T(8,128)(2,1)}, u32[]{:S(2)}) copy-start(bf16[1024,512]{1,0:T(8,128)(2,1)} %param.18) | copy-start | bytes 3145732
  6.5 79.0 %all-gather.5.cloned.1.call-start = ((), (), s32[]{:S(2)}) async-start(), calls=%async_computation.2 | async-start | bytes 1310720 | tf_op jit(solution)/shard_map/all_gather | solution.py:77
  7.3 93.5 %all-gather.7.cloned.1.call-start = ((), (), s32[]{:S(2)}) async-start(), calls=%async_computation.3 | async-start | bytes 1966080 | tf_op jit(solution)/shard_map/all_gather | solution.py:79
  8.0 96.7 %all-gather.9.cloned.1.call-start = ((), (), s32[]{:S(2)}) async-start(), calls=%async_computation.4 | async-start | bytes 1310720 | tf_op jit(solution)/shard_map/all_gather | solution.py:81
  12.0 9.9 %copy-start.15 = (s32[256]{0:T(256)S(1)}, s32[256]{0:T(256)}, u32[]{:S(2)}) copy-start(s32[256]{0:T(256)} %param.24) | copy-start | bytes 3076
  12.0 9.9 %copy-start.6 = (bf16[128,512]{1,0:T(8,128)(2,1)S(1)}, bf16[128,512]{1,0:T(8,128)(2,1)}, u32[]{:S(2)}) copy-start(bf16[128,512]{1,0:T(8,128)(2,1)} %param.26) | copy-start | bytes 393220
  14.8 17.3 %copy-start.7 = (bf16[128,512]{1,0:T(8,128)(2,1)S(1)}, bf16[128,512]{1,0:T(8,128)(2,1)}, u32[]{:S(2)}) copy-start(bf16[128,512]{1,0:T(8,128)(2,1)} %param.27) | copy-start | bytes 393220
  14.8 25.1 %copy-start.8 = (bf16[128,512]{1,0:T(8,128)(2,1)S(1)}, bf16[128,512]{1,0:T(8,128)(2,1)}, u32[]{:S(2)}) copy-start(bf16[128,512]{1,0:T(8,128)(2,1)} %param.29) | copy-start | bytes 393220
  14.8 36.0 %copy-start.9 = (bf16[128,512]{1,0:T(8,128)(2,1)S(1)}, bf16[128,512]{1,0:T(8,128)(2,1)}, u32[]{:S(2)}) copy-start(bf16[128,512]{1,0:T(8,128)(2,1)} %param.31) | copy-start | bytes 393220
  14.8 43.7 %copy-start.10 = (bf16[128,512]{1,0:T(8,128)(2,1)S(1)}, bf16[128,512]{1,0:T(8,128)(2,1)}, u32[]{:S(2)}) copy-start(bf16[128,512]{1,0:T(8,128)(2,1)} %param.33) | copy-start | bytes 393220
  14.9 60.0 %all-to-all-start.1 = ((bf16[4,256,512]{2,1,0:T(8,128)(2,1)}), bf16[4,256,512]{2,1,0:T(8,128)(2,1)S(1)}, u32[]{:S(2)}, u32[]{:S(2)}) async-start(bf16[4,256,512]{2,1,0:T(8,128)(2,1)} %bitcast.4), calls=%async_computation.1 | async-start | bytes 2097152 | tf_op jit(solution)/shard_map/all_to_all | solution.py:105
  21.3 45.7 %copy-start.11 = (bf16[128,512]{1,0:T(8,128)(2,1)S(1)}, bf16[128,512]{1,0:T(8,128)(2,1)}, u32[]{:S(2)}) copy-start(bf16[128,512]{1,0:T(8,128)(2,1)} %param.35) | copy-start | bytes 393220
  21.3 53.4 %copy-start.13 = (s32[256]{0:T(256)S(1)}, s32[256]{0:T(256)}, u32[]{:S(2)}) copy-start(s32[256]{0:T(256)} %param.25) | copy-start | bytes 3076
  21.3 53.4 %copy-start.14 = (s32[1024]{0:T(1024)S(1)}, s32[1024]{0:T(1024)}, u32[]{:S(2)}) copy-start(s32[1024]{0:T(1024)} %param.21) | copy-start | bytes 12292
  21.3 104.1 %all-gather.11.cloned.1.call-start = ((), (), s32[]{:S(2)}) async-start(), calls=%async_computation.5 | async-start | bytes 1310720 | tf_op jit(solution)/shard_map/all_gather | solution.py:83
  74.8 4.7 %copy-start.4 = (bf16[4,256,512]{2,1,0:T(8,128)(2,1)}, bf16[4,256,512]{2,1,0:T(8,128)(2,1)S(1)}, u32[]{:S(2)}) copy-start(bf16[4,256,512]{2,1,0:T(8,128)(2,1)S(1)} %all-to-all-done.1) | copy-start | bytes 3145732
  74.8 10.3 %all-to-all-start = ((s32[4,1,256]{2,1,0:T(1,128)}), s32[4,1,256]{2,1,0:T(1,128)S(1)}, u32[]{:S(2)}, u32[]{:S(2)}) async-start(s32[4,1,256]{2,1,0:T(1,128)} %bitcast.1), calls=%async_computation | async-start | bytes 8192 | tf_op jit(solution)/shard_map/all_to_all | solution.py:112
  82.7 2.9 %copy-start.12 = (bf16[32,512]{1,0:T(8,128)(2,1)S(1)}, bf16[32,512]{1,0:T(8,128)(2,1)}, u32[]{:S(2)}) copy-start(bf16[32,512]{1,0:T(8,128)(2,1)} %param.22) | copy-start | bytes 98308
  93.2 6.3 %collective-permute-start = (bf16[32,512]{1,0:T(8,128)(2,1)S(1)}, bf16[32,512]{1,0:T(8,128)(2,1)S(1)}, u32[]{:S(2)}, u32[]{:S(2)}) collective-permute-start(bf16[32,512]{1,0:T(8,128)(2,1)S(1)} %get-tuple-element.5), channel_id=1, source_target_pairs={{0,4},{4,8},{8,12},{12,0},{1,5},{5,9},{9,13},{13,1},{2,6},{6,10},{... | collective-permute-start | bytes 98312 | tf_op jit(solution)/shard_map/ppermute | solution.py:16
  93.8 5.7 %collective-permute-start.1 = (bf16[32,512]{1,0:T(8,128)(2,1)S(1)}, bf16[32,512]{1,0:T(8,128)(2,1)S(1)}, u32[]{:S(2)}, u32[]{:S(2)}) collective-permute-start(bf16[32,512]{1,0:T(8,128)(2,1)S(1)} %get-tuple-element.6), channel_id=1, source_target_pairs={{4,0},{8,4},{12,8},{0,12},{5,1},{9,5},{13,9},{1,13},{6,2},{10,6},{... | collective-permute-start | bytes 98312 | tf_op jit(solution)/shard_map/ppermute | solution.py:17
  98.4 2.4 %copy-start.5 = (bf16[512,512]{1,0:T(8,128)(2,1)S(1)}, bf16[512,512]{1,0:T(8,128)(2,1)}, u32[]{:S(2)}) copy-start(bf16[512,512]{1,0:T(8,128)(2,1)} %all_gather.42) | copy-start | bytes 1572868
  100.7 4.0 %copy-start.3 = (bf16[512,512]{1,0:T(8,128)(2,1)S(1)}, bf16[512,512]{1,0:T(8,128)(2,1)}, u32[]{:S(2)}) copy-start(bf16[512,512]{1,0:T(8,128)(2,1)} %all_gather.44) | copy-start | bytes 1572868
  129.1 1.2 copy-start.2
Sparse Core Ops, SparseCore 0:
  8.9 20.8 all-gather.4
  31.4 21.9 all-gather.6
  54.9 17.1 all-gather.8
  73.5 16.7 all-gather.10
where the time goes:
time: 139 us
  blocking collectives  70.5 us (51%)
  local copies, waits for them, and re-layouts  16 us (12%)
  starting transfers between devices  15.1 us (11%)
  matrix products  14.7 us (11%)
  between operations  13.4 us (10%)
  waiting for transfers between devices  4.81 us (3%)
  other arithmetic  4.11 us (3%)
    all_gather x1, blocking collectives, per_device(): lane_mesh = lax.all_gather(mesh_out, 'patch', axis=0, tiled=True)  13.5 us
    dot_general x5, matrix products, network(): jnp.dot(hidden, second, preferred_element_type=jnp.float32)  13 us
    all_gather x1, blocking collectives, per_device(): lax.all_gather(gn_w2, ('feat', 'sub'), axis=0, tiled=True)  10.9 us
    all_gather x1, blocking collectives, per_device(): lax.all_gather(enc_w1, ('feat', 'sub'), axis=0, tiled=True)  9.07 us
    all_gather x1, blocking collectives, per_device(): lax.all_gather(node_w2, ('feat', 'sub'), axis=0, tiled=True)  8.41 us
    all_gather x1, blocking collectives, per_device(): lax.all_gather(dec_w2, ('feat', 'sub'), axis=0, tiled=True)  7.74 us
    all_gather x1, blocking collectives, per_device(): lax.all_gather(enc_w2, ('feat', 'sub'), axis=0, tiled=True)  7.74 us
    all_gather x1, blocking collectives, per_device(): lax.all_gather(edge_w2, ('feat', 'sub'), axis=0, tiled=True)  7.73 us
  transfers between devices with their start and end apart: 8, of which 1 were waited for; matrix products, arithmetic and copies ran while one was open for 20% of the time, Pallas kernels for 0%

commit v1 on v0

v1 whole, which is shorter than its diff:
```python
import functools

import jax
import jax.numpy as jnp
from jax import lax
from jax.experimental import pallas as pl
from jax.experimental.pallas import tpu as pltpu
from jax.sharding import PartitionSpec as P

MESH = pl.DeviceIdType.MESH
BF = jnp.bfloat16
F32 = jnp.float32


def dot(a, b):
    return jnp.dot(a, b, preferred_element_type=F32)


def dot_t(a, b):
    return lax.dot_general(a, b, (((0,), (0,)), ((), ())), preferred_element_type=F32)


def silu(u):
    half = 0.5 * u
    return (half + half * jnp.tanh(half)).astype(BF)


def layer_norm(values):
    centred = values - jnp.mean(values, axis=-1, keepdims=True)
    spread = jnp.mean(centred * centred, axis=-1, keepdims=True)
    return centred * lax.rsqrt(spread + 1e-05)


def kernel(sizes, *refs):
    G, NP, F, S = sizes
    L = F * S
    grid_h, owner, enc_node, dec_node, mesh, edge_h, senders, receivers = refs[:8]
    shards = refs[8:18]
    out_h = refs[18]
    full = refs[19:29]
    (
        grid, edge, msgs, outs, part, part_in, ext, lane_p,
        loc_sem, own_sem, w_send, w_recv, p_send, p_recv, m_send, n_send, m_recv, o_send, o_recv, out_sem,
    ) = refs[29:]
    g, p, f, s = (lax.axis_index(a) for a in ("groups", "patch", "feat", "sub"))
    lane = f * S + s
    n_w = len(shards)
    rows, width = grid.shape
    nodes = mesh.shape[0]
    n_edges = edge.shape[0]
    blocks = owner.shape[0]
    blk = rows // blocks
    chunk = 2 * blk
    n_chunks = rows // chunk
    sent = []

    def turn(i, d, n):
        return lax.rem(i + d, n)

    def send(src, dst, ssem, rsem, dev):
        c = pltpu.make_async_remote_copy(
            src_ref=src, dst_ref=dst, send_sem=ssem, recv_sem=rsem, device_id=dev, device_id_type=MESH
        )
        c.start()
        sent.append(c)

    def got(dst, sem):
        pltpu.make_async_copy(dst, dst, sem).wait()

    local = [pltpu.make_async_copy(grid_h, grid, loc_sem.at[0]), pltpu.make_async_copy(edge_h, edge, loc_sem.at[1])]
    for c in local:
        c.start()

    def rows_of(i, ln, h=None):
        r = shards[i].shape[0]
        if h is None:
            return full[i].at[pl.ds(pl.multiple_of(ln * r, 16), r)]
        return full[i].at[pl.ds(pl.multiple_of(ln * r + h * (r // G), 16), r // G)]

    own = [pltpu.make_async_copy(shards[i], rows_of(i, lane), own_sem.at[i]) for i in range(n_w)]
    for c in own:
        c.start()

    barrier = pltpu.get_barrier_semaphore()
    partners = [(turn(g, d, G), p, f, s) for d in range(1, G)]
    partners += [(g, turn(p, d, NP), f, s) for d in range(1, NP)]
    partners += [(g, p, turn(f, df, F), turn(s, ds, S)) for df in range(F) for ds in range(S) if df or ds]
    near = sorted({1 % NP, (NP - 1) % NP} - {0})
    partners += [
        (g, turn(p, d, NP), turn(f, df, F), turn(s, ds, S))
        for d in near for df in range(F) for ds in range(S) if df or ds
    ]
    for dev in partners:
        pl.semaphore_signal(barrier, inc=1, device_id=dev, device_id_type=MESH)
    pl.semaphore_wait(barrier, len(partners))

    slot = [0] * n_w

    def w_out(i, src, dst, rsem, dev):
        send(src, dst, w_send.at[i, slot[i]], rsem, dev)
        slot[i] += 1

    def hop_a(i):
        r = shards[i].shape[0] // G
        for df in range(1, F):
            src = shards[i].at[pl.ds(pl.multiple_of(g * r, 16), r)]
            w_out(i, src, rows_of(i, lane, g), w_recv.at[i, lane, g], (g, p, turn(f, df, F), s))
        for ds in range(1, S):
            w_out(i, shards[i], rows_of(i, lane), w_recv.at[i, lane, 0], (g, p, f, turn(s, ds, S)))

    def hop_b(i):
        for df in range(1, F):
            ln = turn(f, df, F) * S + s
            buf, sem = rows_of(i, ln, g), w_recv.at[i, ln, g]
            got(buf, sem)
            for dg in range(1, G):
                w_out(i, buf, buf, sem, (turn(g, dg, G), p, f, s))
            for ds in range(1, S):
                w_out(i, buf, buf, sem, (g, p, f, turn(s, ds, S)))

    def hop_c(i):
        for df in range(1, F):
            ln = turn(f, df, F) * S + s
            for dg in range(1, G):
                h = turn(g, dg, G)
                buf, sem = rows_of(i, ln, h), w_recv.at[i, ln, h]
                got(buf, sem)
                for ds in range(1, S):
                    w_out(i, buf, buf, sem, (g, p, f, turn(s, ds, S)))

    def hop_d(i):
        own[i].wait()
        for ds in range(1, S):
            so = turn(s, ds, S)
            got(rows_of(i, f * S + so), w_recv.at[i, f * S + so, 0])
            for df in range(1, F):
                ln = turn(f, df, F) * S + so
                for h in range(G):
                    got(rows_of(i, ln, h), w_recv.at[i, ln, h])

    for i in range(n_w):
        hop_a(i)
    hop_b(0)
    hop_b(1)
    hop_c(0)
    hop_c(1)
    hop_b(2)
    hop_d(0)
    hop_d(1)
    local[0].wait()

    between = {0: [lambda: hop_b(3)], 1: [lambda: hop_c(2)], 2: [lambda: hop_c(3)], 3: []}
    for c in range(n_chunks):
        at = pl.ds(c * chunk, chunk)
        h = silu(dot(grid[at, :], full[0][...]))
        msgs[at, :] = layer_norm(dot(h, full[1][...])).astype(BF)
        for step in between.get(c, []):
            step()

    def one_hot(count, first, row):
        ids = lax.broadcasted_iota(jnp.int32, (count, row.shape[1]), 0) + first
        return jnp.where(ids == row, 1.0, 0.0).astype(BF)

    enc_row = jnp.concatenate(
        [enc_node[:, b * blk:(b + 1) * blk] + owner[b] * nodes for b in range(blocks)], axis=1
    )
    dec_row = jnp.concatenate(
        [dec_node[:, b * blk:(b + 1) * blk] + owner[b] * nodes for b in range(blocks)], axis=1
    )
    some = min(NP, 4)
    for q in range(0, NP, some):
        total = dot(one_hot(some * nodes, q * nodes, enc_row), msgs[...])
        part[q * nodes:(q + some) * nodes, :] = total.astype(BF)

    def node_rows(ref, i):
        return ref.at[pl.ds(pl.multiple_of(i * nodes, 16), nodes)]

    for d in range(1, NP):
        q = turn(p, d, NP)
        send(node_rows(part, q), node_rows(part_in, p), p_send.at[d], p_recv.at[p], (g, q, f, s))
    hop_b(4)
    hop_d(2)
    hop_d(3)
    total = part[pl.ds(pl.multiple_of(p * nodes, 16), nodes), :].astype(F32)
    mesh_v = mesh[...]
    u = dot(mesh_v, full[2][:width, :])
    for d in range(1, NP):
        q = turn(p, d, NP)
        got(node_rows(part_in, q), p_recv.at[q])
        total = total + part_in[pl.ds(pl.multiple_of(q * nodes, 16), nodes), :].astype(F32)
    u = u + dot(total.astype(BF), full[2][width:, :])
    mid = (mesh_v.astype(F32) + layer_norm(dot(silu(u), full[3][...]))).astype(BF)
    mine = pl.multiple_of((lane + 1) * nodes, 16)
    ext[pl.ds(mine, nodes), :] = mid
    src = node_rows(ext, lane + 1)
    k = 0
    for df in range(F):
        for ds in range(S):
            if df or ds:
                send(src, src, m_send.at[k], m_recv.at[lane + 1], (g, p, turn(f, df, F), turn(s, ds, S)))
            k += 1

    edge_ends = []
    for want, d, place in ((L - 1, 1, 0), (0, NP - 1, L + 1)):
        copies = []
        k = 0
        for df in range(F):
            for ds in range(S):
                copies.append(
                    pltpu.make_async_remote_copy(
                        src_ref=src, dst_ref=node_rows(ext, place),
                        send_sem=n_send.at[min(place, 1), k], recv_sem=m_recv.at[place],
                        device_id=(g, turn(p, d, NP), df, ds), device_id_type=MESH,
                    )
                )
                k += 1
        edge_ends.append((want, copies))

        @pl.when(lane == want)
        def _():
            for c in copies:
                c.start()

    hop_b(5)
    hop_c(4)
    hop_c(5)
    hop_b(6)
    hop_d(4)
    hop_d(5)
    local[1].wait()
    edge_v = edge[...]
    recv_row = receivers[...]
    recv_hot = one_hot(nodes, 0, recv_row)
    u = dot(edge_v, full[4][:width, :])
    u = u + dot(dot_t(recv_hot, mid).astype(BF), full[4][2 * width:, :])
    for i in range(L + 2):
        @pl.when(lane + 1 != i)
        def _():
            got(node_rows(ext, i), m_recv.at[i])
    hop_b(7)
    send_hot = one_hot((L + 2) * nodes, 0, senders[...])
    u = u + dot(dot_t(send_hot, ext[...]).astype(BF), full[4][width:2 * width, :])
    edge_new = (edge_v.astype(F32) + layer_norm(dot(silu(u), full[5][...]))).astype(BF)
    edge_sum = dot(recv_hot, edge_new).astype(BF)
    hop_c(6)
    hop_c(7)
    hop_b(8)
    hop_d(6)
    hop_d(7)
    u = dot(mid, full[6][:width, :]) + dot(edge_sum, full[6][width:, :])
    mesh_out = (mid.astype(F32) + layer_norm(dot(silu(u), full[7][...]))).astype(BF)
    hop_b(9)
    hop_c(8)
    hop_c(9)
    hop_d(8)
    lane_p[pl.ds(pl.multiple_of(p * nodes, 16), nodes), :] = dot(mesh_out, full[8][width:, :]).astype(BF)
    for d in range(1, NP):
        send(node_rows(lane_p, p), node_rows(lane_p, p), o_send.at[d], o_recv.at[p], (g, turn(p, d, NP), f, s))
    hop_d(9)
    for d in range(1, NP):
        q = turn(p, d, NP)
        got(node_rows(lane_p, q), o_recv.at[q])

    leave = []
    for c in range(n_chunks):
        at = pl.ds(c * chunk, chunk)
        hot = one_hot(NP * nodes, 0, dec_row[:, c * chunk:(c + 1) * chunk])
        u = dot(grid[at, :], full[8][:width, :]) + dot_t(hot, lane_p[...])
        res = grid[at, :].astype(F32) + layer_norm(dot(silu(u), full[9][...]))
        outs[at, :] = res.astype(BF)
        copy = pltpu.make_async_copy(outs.at[at], out_h.at[at], out_sem.at[c])
        copy.start()
        leave.append(copy)

    for c in sent:
        c.wait_send()
    for want, copies in edge_ends:
        @pl.when(lane == want)
        def _():
            for c in copies:
                c.wait_send()
    for c in leave:
        c.wait()


def per_device(
    sizes, grid_feat, block_owner, enc_node, dec_node, mesh_feat, edge_feat, senders, receivers, *weights
):
    G, NP, F, S = sizes
    L = F * S
    rows, width = grid_feat.shape
    nodes = mesh_feat.shape[0]
    n_edges = edge_feat.shape[0]
    n_w = len(weights)
    any_spec = pl.BlockSpec(memory_space=pl.ANY)
    vmem = pl.BlockSpec(memory_space=pltpu.VMEM)
    smem = pl.BlockSpec(memory_space=pltpu.SMEM)
    dma = pltpu.SemaphoreType.DMA
    hops = (S - 1) + (F - 1) * (1 + (G - 1) + (S - 1) + (G - 1) * (S - 1))
    n_chunks = block_owner.shape[0] // 2
    scratch = [pltpu.VMEM((w.shape[0] * L, w.shape[1]), BF) for w in weights] + [
        pltpu.VMEM((rows, width), BF),
        pltpu.VMEM((n_edges, width), BF),
        pltpu.VMEM((rows, width), BF),
        pltpu.VMEM((rows, width), BF),
        pltpu.VMEM((NP * nodes, width), BF),
        pltpu.VMEM((NP * nodes, width), BF),
        pltpu.VMEM(((L + 2) * nodes, width), BF),
        pltpu.VMEM((NP * nodes, width), BF),
        dma((2,)),
        dma((n_w,)),
        dma((n_w, hops)),
        dma((n_w, L, G)),
        dma((NP,)),
        dma((NP,)),
        dma((L,)),
        dma((2, L)),
        dma((L + 2,)),
        dma((NP,)),
        dma((NP,)),
        dma((n_chunks,)),
    ]
    return pl.pallas_call(
        functools.partial(kernel, sizes),
        out_shape=jax.ShapeDtypeStruct((rows, width), BF),
        in_specs=[any_spec, smem, vmem, vmem, vmem, any_spec, vmem, vmem] + [any_spec] * n_w,
        out_specs=any_spec,
        scratch_shapes=scratch,
        compiler_params=pltpu.CompilerParams(
            collective_id=0, has_side_effects=True, vmem_limit_bytes=56 * 1024 * 1024
        ),
    )(
        grid_feat, block_owner, enc_node.reshape(1, -1), dec_node.reshape(1, -1), mesh_feat, edge_feat,
        senders.reshape(1, -1), receivers.reshape(1, -1), *weights
    )


def solution(mesh):
    every = ("groups", "patch", "feat", "sub")
    sizes = tuple(mesh.shape[a] for a in every)
    row, vec, weight = P(every, None), P(every), P(("feat", "sub"), None)
    in_specs = (row, vec, vec, vec, row, row, vec, vec) + (weight,) * 10
    return jax.shard_map(
        functools.partial(per_device, sizes), mesh=mesh, in_specs=in_specs, out_specs=row, check_vma=False
    )
```

time: 139 us -> 54.8 us (0.39)
  blocking collectives: 70.5 us -> 0 us
  Pallas kernels: 0 us -> 52.3 us
  starting transfers between devices: 15.1 us -> 0 us
  matrix products: 14.7 us -> 0 us
  local copies, waits for them, and re-layouts: 16 us -> 2.26 us
  between operations: 13.4 us -> 0.01 us
  waiting for transfers between devices: 4.81 us -> 0 us
  other arithmetic: 4.11 us -> 0 us
    all_gather x8 -> x0, blocking collectives: 70.5 us -> none  [the longest x1 13.5 us: per_device(): lane_mesh = lax.all_gather(mesh_out, 'patch', axis=0, tiled=True)]
    pallas_call x0 -> x1, Pallas kernels: none -> 52.3 us  [per_device(): pl.pallas_call(functools.partial(kernel, sizes), out_shape=jax.ShapeDtype...]
    dot_general x7 -> x0, matrix products: 14.7 us -> none  [the longest x5 13 us: network(): jnp.dot(hidden, second, preferred_element_type=jnp.float32)]
    all_to_all x2 -> x0, starting transfers between devices: 11.2 us -> none  [the longest x1 6.46 us: per_device(): lax.all_to_all(buffer.reshape(patch_count, capacity * block_rows, width),...]
    gather x3 -> x0, local copies, waits for them, and re-layouts: 7.35 us -> none  [the longest x1 5.05 us: per_device(): decoder_in = jnp.concatenate([grid_feat, lane_mesh[source]], 1)]
    scatter x2 -> x0, local copies, waits for them, and re-layouts: 4.01 us -> none  [the longest x1 2.85 us: per_device(): buffer = jnp.zeros((patch_count * capacity, block_rows, width), jnp.bfloa...]
    ppermute x2 -> x0, starting transfers between devices: 3.84 us -> none  [the longest x1 3.25 us: extended_2(): after = lax.ppermute(first, axis, down)]
    unnamed x4 -> x0, waiting for transfers between devices: 2.61 us -> none
  transfers between devices with their start and end apart: 8 -> 0, of which waited for: 1 -> 0; matrix products, arithmetic and copies ran while one was open for 20% -> 0% of each run, Pallas kernels for 0% -> 0%
where the time goes in v1:
time: 54.8 us; the launch traced here: 54.6 us
  Pallas kernels  52.3 us (95%)
  local copies, waits for them, and re-layouts  2.26 us (4%)
    pallas_call x1, Pallas kernels, per_device(): pl.pallas_call(functools.partial(kernel, sizes), out_shape=jax.ShapeDtype...  52.3 us
    unnamed x1, local copies, waits for them, and re-layouts  2.26 us

profile of v1, /device:TPU:0, one launch (start us, length us, event | category | flops | bytes accessed | tf_op | source)
XLA Modules:
  0.0 54.6 jit_solution(17829608889712288812)
XLA Ops:
  0.0 52.3 %shard_map.172 = bf16[1024,512]{1,0:T(8,128)(2,1)} custom-call(bf16[1024,512]{1,0:T(8,128)(2,1)} %refs_0_.1, s32[8]{0:T(128)} %refs_1_.1, s32[1,1024]{1,0:T(1,128)} %bitcast.4, s32[1,1024]{1,0:T(1,128)} %bitcast.5, bf16[32,512]{1,0:T(8,128)(2,1)} %refs_4_.1, bf16[256,512]{1,0:T(8,128)(2,1)} %refs_5_.1, s32[1,256]{1,0:T(1,128)} %bitcast.6, s32[1,256]{1,0:T(1,128)} %bitcast.7, ...), custom_call_target="tpu_custom_call" | custom-call | tf_op jit(solution)/shard_map/pallas_call | solution.py:323
  52.3 2.3 %copy.20 = bf16[1024,512]{1,0:T(8,128)(2,1)} copy(bf16[1024,512]{1,0:T(8,128)(2,1)} %shard_map.172) | data formatting | bytes 2097152

commit v2 on v1

--- a/solution.py
+++ b/solution.py
@@ -39,8 +39,8 @@
     out_h = refs[18]
     full = refs[19:29]
     (
-        grid, edge, msgs, outs, part, part_in, ext, lane_p,
-        loc_sem, own_sem, w_send, w_recv, p_send, p_recv, m_send, n_send, m_recv, o_send, o_recv, out_sem,
+        grid, edge, msgs, outs, ahead, part, part_in, ext, lane_p,
+        loc_sem, own_sem, w_send, w_recv, p_send, p_recv, m_send, n_send, m_recv, o_send, o_recv, out_sem, relay_sem,
     ) = refs[29:]
     g, p, f, s = (lax.axis_index(a) for a in ("groups", "patch", "feat", "sub"))
     lane = f * S + s
@@ -71,28 +71,47 @@
     for c in local:
         c.start()
 
+    pairs = ([(g, (1 - g, p, f, s))] if G == 2 else []) + (
+        [(lax.rem(p, 2), (g, p + 1 - 2 * lax.rem(p, 2), f, s))] if NP % 2 == 0 else []
+    )
+    cuts = 2 if pairs else 1
+
+    def half_of(i):
+        return pairs[i % len(pairs)][0] if pairs else 0
+
     def rows_of(i, ln, h=None):
         r = shards[i].shape[0]
         if h is None:
             return full[i].at[pl.ds(pl.multiple_of(ln * r, 16), r)]
-        return full[i].at[pl.ds(pl.multiple_of(ln * r + h * (r // G), 16), r // G)]
+        return full[i].at[pl.ds(pl.multiple_of(ln * r + h * (r // cuts), 16), r // cuts)]
 
     own = [pltpu.make_async_copy(shards[i], rows_of(i, lane), own_sem.at[i]) for i in range(n_w)]
     for c in own:
         c.start()
 
     barrier = pltpu.get_barrier_semaphore()
-    partners = [(turn(g, d, G), p, f, s) for d in range(1, G)]
-    partners += [(g, turn(p, d, NP), f, s) for d in range(1, NP)]
-    partners += [(g, p, turn(f, df, F), turn(s, ds, S)) for df in range(F) for ds in range(S) if df or ds]
-    near = sorted({1 % NP, (NP - 1) % NP} - {0})
-    partners += [
-        (g, turn(p, d, NP), turn(f, df, F), turn(s, ds, S))
-        for d in near for df in range(F) for ds in range(S) if df or ds
-    ]
-    for dev in partners:
+    near = [(turn(g, d, G), p, f, s) for d in range(1, G)]
+    near += [(g, p, turn(f, df, F), turn(s, ds, S)) for df in range(F) for ds in range(S) if df or ds]
+    line = ((p < NP - 1, (g, lax.min(p + 1, NP - 1), f, s)), (p > 0, (g, lax.max(p - 1, 0), f, s)))
+    for dev in near:
         pl.semaphore_signal(barrier, inc=1, device_id=dev, device_id_type=MESH)
-    pl.semaphore_wait(barrier, len(partners))
+    for there, dev in line:
+        @pl.when(there)
+        def _():
+            pl.semaphore_signal(barrier, inc=1, device_id=dev, device_id_type=MESH)
+    pl.semaphore_wait(barrier, len(near) + sum(there.astype(jnp.int32) for there, _ in line))
+
+    def relay():
+        for k in range(2):
+            (there, dev), (back, _) = line[k], line[1 - k]
+
+            @pl.when(back)
+            def _():
+                pl.semaphore_wait(relay_sem.at[k], 1)
+
+            @pl.when(there)
+            def _():
+                pl.semaphore_signal(relay_sem.at[k], inc=1, device_id=dev, device_id_type=MESH)
 
     slot = [0] * n_w
 
@@ -101,32 +120,35 @@
         slot[i] += 1
 
     def hop_a(i):
-        r = shards[i].shape[0] // G
+        r = shards[i].shape[0] // cuts
+        h = half_of(i)
         for df in range(1, F):
-            src = shards[i].at[pl.ds(pl.multiple_of(g * r, 16), r)]
-            w_out(i, src, rows_of(i, lane, g), w_recv.at[i, lane, g], (g, p, turn(f, df, F), s))
+            src = shards[i].at[pl.ds(pl.multiple_of(h * r, 16), r)]
+            w_out(i, src, rows_of(i, lane, h), w_recv.at[i, lane, h], (g, p, turn(f, df, F), s))
         for ds in range(1, S):
             w_out(i, shards[i], rows_of(i, lane), w_recv.at[i, lane, 0], (g, p, f, turn(s, ds, S)))
 
     def hop_b(i):
+        h = half_of(i)
         for df in range(1, F):
             ln = turn(f, df, F) * S + s
-            buf, sem = rows_of(i, ln, g), w_recv.at[i, ln, g]
+            buf, sem = rows_of(i, ln, h), w_recv.at[i, ln, h]
             got(buf, sem)
-            for dg in range(1, G):
-                w_out(i, buf, buf, sem, (turn(g, dg, G), p, f, s))
+            if pairs:
+                w_out(i, buf, buf, sem, pairs[i % len(pairs)][1])
             for ds in range(1, S):
                 w_out(i, buf, buf, sem, (g, p, f, turn(s, ds, S)))
 
     def hop_c(i):
+        if not pairs:
+            return
+        h = 1 - half_of(i)
         for df in range(1, F):
             ln = turn(f, df, F) * S + s
-            for dg in range(1, G):
-                h = turn(g, dg, G)
-                buf, sem = rows_of(i, ln, h), w_recv.at[i, ln, h]
-                got(buf, sem)
-                for ds in range(1, S):
-                    w_out(i, buf, buf, sem, (g, p, f, turn(s, ds, S)))
+            buf, sem = rows_of(i, ln, h), w_recv.at[i, ln, h]
+            got(buf, sem)
+            for ds in range(1, S):
+                w_out(i, buf, buf, sem, (g, p, f, turn(s, ds, S)))
 
     def hop_d(i):
         own[i].wait()
@@ -135,21 +157,22 @@
             got(rows_of(i, f * S + so), w_recv.at[i, f * S + so, 0])
             for df in range(1, F):
                 ln = turn(f, df, F) * S + so
-                for h in range(G):
+                for h in range(cuts):
                     got(rows_of(i, ln, h), w_recv.at[i, ln, h])
 
     for i in range(n_w):
         hop_a(i)
+    relay()
     hop_b(0)
     hop_b(1)
     hop_c(0)
+    hop_b(2)
     hop_c(1)
-    hop_b(2)
     hop_d(0)
     hop_d(1)
     local[0].wait()
 
-    between = {0: [lambda: hop_b(3)], 1: [lambda: hop_c(2)], 2: [lambda: hop_c(3)], 3: []}
+    between = {n_chunks // 2 - 1: [lambda: hop_b(3), lambda: hop_c(2)], n_chunks - 1: [lambda: hop_c(3)]}
     for c in range(n_chunks):
         at = pl.ds(c * chunk, chunk)
         h = silu(dot(grid[at, :], full[0][...]))
@@ -181,6 +204,8 @@
     hop_b(4)
     hop_d(2)
     hop_d(3)
+    hop_b(5)
+    hop_c(4)
     total = part[pl.ds(pl.multiple_of(p * nodes, 16), nodes), :].astype(F32)
     mesh_v = mesh[...]
     u = dot(mesh_v, full[2][:width, :])
@@ -221,52 +246,57 @@
             for c in copies:
                 c.start()
 
-    hop_b(5)
-    hop_c(4)
+    hop_b(6)
     hop_c(5)
-    hop_b(6)
     hop_d(4)
-    hop_d(5)
     local[1].wait()
     edge_v = edge[...]
     recv_row = receivers[...]
     recv_hot = one_hot(nodes, 0, recv_row)
     u = dot(edge_v, full[4][:width, :])
     u = u + dot(dot_t(recv_hot, mid).astype(BF), full[4][2 * width:, :])
+    hop_b(7)
+    hop_c(6)
+    hop_d(5)
     for i in range(L + 2):
         @pl.when(lane + 1 != i)
         def _():
             got(node_rows(ext, i), m_recv.at[i])
-    hop_b(7)
     send_hot = one_hot((L + 2) * nodes, 0, senders[...])
     u = u + dot(dot_t(send_hot, ext[...]).astype(BF), full[4][width:2 * width, :])
-    edge_new = (edge_v.astype(F32) + layer_norm(dot(silu(u), full[5][...]))).astype(BF)
+    h = silu(u)
+    edge_new = (edge_v.astype(F32) + layer_norm(dot(h, full[5][...]))).astype(BF)
     edge_sum = dot(recv_hot, edge_new).astype(BF)
-    hop_c(6)
+    hop_b(8)
     hop_c(7)
-    hop_b(8)
     hop_d(6)
     hop_d(7)
     u = dot(mid, full[6][:width, :]) + dot(edge_sum, full[6][width:, :])
-    mesh_out = (mid.astype(F32) + layer_norm(dot(silu(u), full[7][...]))).astype(BF)
+    h = silu(u)
+    mesh_out = (mid.astype(F32) + layer_norm(dot(h, full[7][...]))).astype(BF)
+    lane_p[pl.ds(pl.multiple_of(p * nodes, 16), nodes), :] = mesh_out
+    for d in range(1, NP):
+        send(node_rows(lane_p, p), node_rows(lane_p, p), o_send.at[d], o_recv.at[p], (g, turn(p, d, NP), f, s))
     hop_b(9)
     hop_c(8)
+    hop_d(8)
+    for c in range(n_chunks):
+        at = pl.ds(c * chunk, chunk)
+        ahead[at, :] = dot(grid[at, :], full[8][:width, :])
     hop_c(9)
-    hop_d(8)
-    lane_p[pl.ds(pl.multiple_of(p * nodes, 16), nodes), :] = dot(mesh_out, full[8][width:, :]).astype(BF)
-    for d in range(1, NP):
-        send(node_rows(lane_p, p), node_rows(lane_p, p), o_send.at[d], o_recv.at[p], (g, turn(p, d, NP), f, s))
     hop_d(9)
     for d in range(1, NP):
         q = turn(p, d, NP)
         got(node_rows(lane_p, q), o_recv.at[q])
 
     leave = []
+
+    lane_part = dot(lane_p[...], full[8][width:, :]).astype(BF)
     for c in range(n_chunks):
         at = pl.ds(c * chunk, chunk)
         hot = one_hot(NP * nodes, 0, dec_row[:, c * chunk:(c + 1) * chunk])
-        u = dot(grid[at, :], full[8][:width, :]) + dot_t(hot, lane_p[...])
-        res = grid[at, :].astype(F32) + layer_norm(dot(silu(u), full[9][...]))
+        h = silu(ahead[at, :] + dot_t(hot, lane_part))
+        res = grid[at, :].astype(F32) + layer_norm(dot(h, full[9][...]))
         outs[at, :] = res.astype(BF)
         copy = pltpu.make_async_copy(outs.at[at], out_h.at[at], out_sem.at[c])
         copy.start()
@@ -296,13 +326,14 @@
     vmem = pl.BlockSpec(memory_space=pltpu.VMEM)
     smem = pl.BlockSpec(memory_space=pltpu.SMEM)
     dma = pltpu.SemaphoreType.DMA
-    hops = (S - 1) + (F - 1) * (1 + (G - 1) + (S - 1) + (G - 1) * (S - 1))
+    hops = (S - 1) + (F - 1) * (2 + 2 * (S - 1))
     n_chunks = block_owner.shape[0] // 2
     scratch = [pltpu.VMEM((w.shape[0] * L, w.shape[1]), BF) for w in weights] + [
         pltpu.VMEM((rows, width), BF),
         pltpu.VMEM((n_edges, width), BF),
         pltpu.VMEM((rows, width), BF),
         pltpu.VMEM((rows, width), BF),
+        pltpu.VMEM((rows, width), F32),
         pltpu.VMEM((NP * nodes, width), BF),
         pltpu.VMEM((NP * nodes, width), BF),
         pltpu.VMEM(((L + 2) * nodes, width), BF),
@@ -310,7 +341,7 @@
         dma((2,)),
         dma((n_w,)),
         dma((n_w, hops)),
-        dma((n_w, L, G)),
+        dma((n_w, L, 2)),
         dma((NP,)),
         dma((NP,)),
         dma((L,)),
@@ -319,6 +350,7 @@
         dma((NP,)),
         dma((NP,)),
         dma((n_chunks,)),
+        pltpu.SemaphoreType.REGULAR((2,)),
     ]
     return pl.pallas_call(
         functools.partial(kernel, sizes),

time: 54.8 us -> 47.7 us (0.87)
  Pallas kernels: 52.3 us -> 45.2 us
    pallas_call x1, Pallas kernels: 52.3 us -> 45.2 us  [per_device(): pl.pallas_call(functools.partial(kernel, sizes), out_shape=jax.ShapeDtype...]
where the time goes in v2:
time: 47.7 us; the launch traced here: 47.5 us
  Pallas kernels  45.2 us (95%)
  local copies, waits for them, and re-layouts  2.26 us (5%)
    pallas_call x1, Pallas kernels, per_device(): pl.pallas_call(functools.partial(kernel, sizes), out_shape=jax.ShapeDtype...  45.2 us
    unnamed x1, local copies, waits for them, and re-layouts  2.26 us

profile of v2, /device:TPU:0, one launch (start us, length us, event | category | flops | bytes accessed | tf_op | source)
XLA Modules:
  0.0 47.5 jit_solution(7209587557890047049)
XLA Ops:
  0.0 45.2 %shard_map.172 = bf16[1024,512]{1,0:T(8,128)(2,1)} custom-call(bf16[1024,512]{1,0:T(8,128)(2,1)} %refs_0_.1, s32[8]{0:T(128)} %refs_1_.1, s32[1,1024]{1,0:T(1,128)} %bitcast.4, s32[1,1024]{1,0:T(1,128)} %bitcast.5, bf16[32,512]{1,0:T(8,128)(2,1)} %refs_4_.1, bf16[256,512]{1,0:T(8,128)(2,1)} %refs_5_.1, s32[1,256]{1,0:T(1,128)} %bitcast.6, s32[1,256]{1,0:T(1,128)} %bitcast.7, ...), custom_call_target="tpu_custom_call" | custom-call | tf_op jit(solution)/shard_map/pallas_call | solution.py:355
  45.2 2.3 %copy.20 = bf16[1024,512]{1,0:T(8,128)(2,1)} copy(bf16[1024,512]{1,0:T(8,128)(2,1)} %shard_map.172) | data formatting | bytes 2097152

commit v3 on v2

--- a/solution.py
+++ b/solution.py
@@ -172,7 +172,7 @@
     hop_d(1)
     local[0].wait()
 
-    between = {n_chunks // 2 - 1: [lambda: hop_b(3), lambda: hop_c(2)], n_chunks - 1: [lambda: hop_c(3)]}
+    between = {n_chunks // 2 - 1: [lambda: hop_b(3), lambda: hop_c(2)], n_chunks - 1: [lambda: hop_c(3), lambda: hop_b(4)]}
     for c in range(n_chunks):
         at = pl.ds(c * chunk, chunk)
         h = silu(dot(grid[at, :], full[0][...]))
@@ -201,11 +201,11 @@
     for d in range(1, NP):
         q = turn(p, d, NP)
         send(node_rows(part, q), node_rows(part_in, p), p_send.at[d], p_recv.at[p], (g, q, f, s))
-    hop_b(4)
     hop_d(2)
     hop_d(3)
     hop_b(5)
     hop_c(4)
+    hop_b(6)
     total = part[pl.ds(pl.multiple_of(p * nodes, 16), nodes), :].astype(F32)
     mesh_v = mesh[...]
     u = dot(mesh_v, full[2][:width, :])
@@ -246,8 +246,8 @@
             for c in copies:
                 c.start()
 
-    hop_b(6)
     hop_c(5)
+    hop_b(7)
     hop_d(4)
     local[1].wait()
     edge_v = edge[...]
@@ -255,9 +255,9 @@
     recv_hot = one_hot(nodes, 0, recv_row)
     u = dot(edge_v, full[4][:width, :])
     u = u + dot(dot_t(recv_hot, mid).astype(BF), full[4][2 * width:, :])
-    hop_b(7)
     hop_c(6)
     hop_d(5)
+    hop_b(8)
     for i in range(L + 2):
         @pl.when(lane + 1 != i)
         def _():
@@ -267,8 +267,9 @@
     h = silu(u)
     edge_new = (edge_v.astype(F32) + layer_norm(dot(h, full[5][...]))).astype(BF)
     edge_sum = dot(recv_hot, edge_new).astype(BF)
-    hop_b(8)
     hop_c(7)
+    hop_b(9)
+    hop_c(8)
     hop_d(6)
     hop_d(7)
     u = dot(mid, full[6][:width, :]) + dot(edge_sum, full[6][width:, :])
@@ -277,13 +278,11 @@
     lane_p[pl.ds(pl.multiple_of(p * nodes, 16), nodes), :] = mesh_out
     for d in range(1, NP):
         send(node_rows(lane_p, p), node_rows(lane_p, p), o_send.at[d], o_recv.at[p], (g, turn(p, d, NP), f, s))
-    hop_b(9)
-    hop_c(8)
+    hop_c(9)
     hop_d(8)
     for c in range(n_chunks):
         at = pl.ds(c * chunk, chunk)
         ahead[at, :] = dot(grid[at, :], full[8][:width, :])
-    hop_c(9)
     hop_d(9)
     for d in range(1, NP):
         q = turn(p, d, NP)

time: 47.7 us -> 45.8 us (0.960)
  Pallas kernels: 45.2 us -> 43.3 us
    pallas_call x1, Pallas kernels: 45.2 us -> 43.3 us  [per_device(): pl.pallas_call(functools.partial(kernel, sizes), out_shape=jax.ShapeDtype...]
where the time goes in v3:
time: 45.8 us; the launch traced here: 45.6 us
  Pallas kernels  43.3 us (95%)
  local copies, waits for them, and re-layouts  2.26 us (5%)
    pallas_call x1, Pallas kernels, per_device(): pl.pallas_call(functools.partial(kernel, sizes), out_shape=jax.ShapeDtype...  43.3 us
    unnamed x1, local copies, waits for them, and re-layouts  2.26 us

profile of v3, /device:TPU:0, one launch (start us, length us, event | category | flops | bytes accessed | tf_op | source)
XLA Modules:
  0.0 45.6 jit_solution(8329315252289206311)
XLA Ops:
  0.0 43.3 %shard_map.172 = bf16[1024,512]{1,0:T(8,128)(2,1)} custom-call(bf16[1024,512]{1,0:T(8,128)(2,1)} %refs_0_.1, s32[8]{0:T(128)} %refs_1_.1, s32[1,1024]{1,0:T(1,128)} %bitcast.4, s32[1,1024]{1,0:T(1,128)} %bitcast.5, bf16[32,512]{1,0:T(8,128)(2,1)} %refs_4_.1, bf16[256,512]{1,0:T(8,128)(2,1)} %refs_5_.1, s32[1,256]{1,0:T(1,128)} %bitcast.6, s32[1,256]{1,0:T(1,128)} %bitcast.7, ...), custom_call_target="tpu_custom_call" | custom-call | tf_op jit(solution)/shard_map/pallas_call | solution.py:354
  43.3 2.3 %copy.20 = bf16[1024,512]{1,0:T(8,128)(2,1)} copy(bf16[1024,512]{1,0:T(8,128)(2,1)} %shard_map.172) | data formatting | bytes 2097152
